TPU v7x, 256 devices: a whole 4x4x8 slice. The times are simulated.
256 devices in a mesh: section: 16 (over y, z_hi), peer: 16 (over x, z_lo, core).
Axes of the slice: x: 4, y: 4, z: 8 (z_hi: 4, z_lo: 2; z = z_hi * 2 + z_lo), core: 2. Of those that a mesh axis runs over, the one named last changes fastest.
Arguments:
- acts_fwd: bfloat16 [16, 4096, 2560], P('section', 'peer'), may hold values from -30 to 30
- acts_bwd: bfloat16 [16, 4096, 2560], P('section', 'peer'), may hold values from -30 to 30
- cot_bwd: bfloat16 [16, 4096, 2560], P('section', 'peer'), may hold values from -6 to 6
- gain: float32 [16, 2560], P('section'), may hold values from 0.1 to 1.9
- proj: bfloat16 [16, 2560, 2560], P('section', 'peer'), may hold values from -0.125 to 0.125
- fwd_route: int32 [16, 256, 1], P('section', 'peer'), may hold values from 0 to 15; in each aligned block of 16 rows (0 to 15, 16 to 31, ..., all dimensions but the last counted through in order) no two rows name the same one
- bwd_route: int32 [16, 256, 1], P('section', 'peer'), may hold values from 0 to 15; in each aligned block of 16 rows (0 to 15, 16 to 31, ..., all dimensions but the last counted through in order) no two rows name the same one
- straggler: int32 [16, 16], P('section'), may hold values from 0 to 1, as said below
Outputs:
- next_acts: bfloat16 [16, 4096, 2560], P('section', 'peer')
- back_grads: bfloat16 [16, 4096, 2560], P('section', 'peer')
- weight_gradient_mean: float32 [16, 2560, 2560], P('section', 'peer')
Inputs may be any that keep to these rules, and one draw needn't show every extreme that they name: `fwd_route`: among the 16 blocks of one peer of one section, every peer index appears exactly 1 times. `bwd_route`: among the 16 blocks of one peer of one section, every peer index appears exactly 1 times. `straggler`: in every section at least one peer is not excluded.
All inputs are finite; a program needn't handle non-finite values.
Results may differ from a plain program's by a relative error of at most 0.019.
Values may be sent and summed in bfloat16 or wider, within the bound.
A program may use at most 192 MiB of HBM per device.

v0:
```python
import jax
import jax.numpy as jnp
from jax import lax
from jax.sharding import PartitionSpec as P

epsilon = 1e-05


def shifted(x, axis, by):
    size = lax.axis_size(axis)
    pairs = [(i, i + by) for i in range(size) if 0 <= i + by < size]
    return lax.ppermute(x, axis, pairs)


def normalize(values, gain_row):
    wide_vals = values.astype(jnp.float32)
    scale_row = lax.rsqrt(jnp.mean(wide_vals * wide_vals, axis=-1, keepdims=True) + epsilon)
    return (wide_vals, scale_row, (wide_vals * scale_row * gain_row).astype(jnp.bfloat16))


def deal_blocks(section_rows, route_table, peer_count):
    block_count = route_table.shape[0]
    slot_count = block_count // peer_count
    channels = section_rows.shape[1]
    block_rows = section_rows.shape[0] // block_count
    same_dest = route_table[:, None] == route_table[None, :]
    earlier = jnp.arange(block_count)[:, None] > jnp.arange(block_count)[None, :]
    slot_rank = jnp.sum((same_dest & earlier).astype(jnp.int32), axis=1)
    dest_ids = jnp.arange(peer_count, dtype=jnp.int32)
    slot_ids = jnp.arange(slot_count, dtype=jnp.int32)
    picked = (route_table[None, None, :] == dest_ids[:, None, None]) & (
        slot_rank[None, None, :] == slot_ids[None, :, None]
    )
    selector = picked.astype(jnp.bfloat16)
    flat_blocks = section_rows.reshape(block_count, block_rows * channels)
    dealt = jnp.einsum("dcj,jm->dcm", selector, flat_blocks, preferred_element_type=jnp.float32)
    return dealt.astype(jnp.bfloat16).reshape(peer_count, slot_count * block_rows, channels)


def local(acts_fwd, acts_bwd, cot_bwd, gain, proj, fwd_route, bwd_route, straggler):
    peer_count = lax.axis_size("peer")
    my_peer = lax.axis_index("peer")
    acts_a = acts_fwd[0]
    acts_b = acts_bwd[0]
    cot_b = cot_bwd[0]
    gain_row = gain[0]
    row_total = acts_a.shape[0]
    channels = acts_a.shape[1]
    wide_a, scale_a, normed_a = normalize(acts_a, gain_row)
    wide_b, scale_b, normed_b = normalize(acts_b, gain_row)
    piece_rows = lax.all_gather(proj, "peer", axis=1, tiled=True)[0]
    columns = normed_a
    hidden_sum = jnp.dot(columns, piece_rows, preferred_element_type=jnp.float32)
    partial_value = lax.dot_general(
        cot_b, piece_rows, (((1,), (1,)), ((), ())), preferred_element_type=jnp.float32
    )
    out_a = (wide_a + hidden_sum).astype(jnp.bfloat16)
    cot_wide = cot_b.astype(jnp.float32)
    scaled = gain_row * partial_value
    inner = jnp.mean(wide_b * scaled, axis=-1, keepdims=True)
    grad_in = (cot_wide + scale_b * scaled - wide_b * scale_b * scale_b * scale_b * inner).astype(
        jnp.bfloat16
    )
    keep_every_peer = 1.0 - straggler[0].astype(jnp.float32)
    remaining_peers = jnp.sum(keep_every_peer)
    keep_mine = jnp.sum(
        keep_every_peer * (jnp.arange(peer_count, dtype=jnp.int32) == my_peer).astype(jnp.float32)
    )
    columns = normed_b
    product = lax.dot_general(
        columns, cot_b, (((0,), (0,)), ((), ())), preferred_element_type=jnp.float32
    )
    gradient_total = lax.psum_scatter(
        (keep_mine * product).astype(jnp.bfloat16), "peer", scatter_dimension=0, tiled=True
    ).astype(jnp.float32)
    weight_gradient_mean = (gradient_total / remaining_peers)[None]
    send_up = deal_blocks(out_a, fwd_route[0, :, 0], peer_count)
    send_down = deal_blocks(grad_in, bwd_route[0, :, 0], peer_count)
    dealt_up, dealt_down = (
        lax.all_to_all(send_up, "peer", split_axis=0, concat_axis=0, tiled=True),
        lax.all_to_all(send_down, "peer", split_axis=0, concat_axis=0, tiled=True),
    )
    landed_up = shifted(dealt_up, "section", 1)
    landed_down = shifted(dealt_down, "section", -1)
    next_acts = landed_up.reshape(1, row_total, channels)
    back_grads = landed_down.reshape(1, row_total, channels)
    return (next_acts, back_grads, weight_gradient_mean)


def solution(mesh):
    in_specs = (
        P("section", "peer", None),
        P("section", "peer", None),
        P("section", "peer", None),
        P("section", None),
        P("section", "peer", None),
        P("section", "peer", None),
        P("section", "peer", None),
        P("section", None),
    )
    out_specs = (P("section", "peer", None), P("section", "peer", None), P("section", "peer", None))
    return jax.shard_map(local, mesh=mesh, in_specs=in_specs, out_specs=out_specs, check_vma=False)
```

profile of v0, /device:TPU:49, one launch (start us, length us, event | category | flops | bytes accessed | tf_op | source)
XLA Modules:
  0.0 372.9 jit_solution(4787697015753343515)
XLA Ops:
  7.2 0.0 all-gather.2.cloned.1.call-start
  7.2 0.7 all-gather.2.cloned.1.call-update
  7.9 0.0 reduce-scatter.2.cloned.1.call-start
  7.9 0.7 reduce.1
  8.7 1.3 fusion.51
  10.0 0.0 copy-start.3
  10.0 0.0 copy-start.5
  10.0 79.6 %all-gather.2.cloned.1.call-done = bf16[1,2560,2560]{2,1,0:T(8,128)(2,1)} async-done(((bf16[1,160,2560]{2,1,0:T(8,128)(2,1)}), bf16[1,2560,2560]{2,1,0:T(8,128)(2,1)}) %all-gather.2.cloned.1.call-update) | async-done | bytes 13107216 | tf_op jit(solution)/shard_map/all_gather | solution.py:51
  89.6 10.5 %fusion.20 = (f32[256]{0:T(256)S(1)}, f32[256]{0:T(256)S(1)}, f32[256,2560]{1,0:T(8,128)}) fusion(bf16[1,256,2560]{2,1,0:T(8,128)(2,1)} %param.9, bf16[1,2560,2560]{2,1,0:T(8,128)(2,1)} %all-gather.2.cloned.1.call-done, bf16[1,256,2560]{2,1,0:T(8,128)(2,1)} %param.10, f32[2560]{0:T(1024)S(1)} %reduce.1), kind=kOutput, calls=%fused_computation.21 | convolution fusion | flops 3359374848 | bytes 18362368 | tf_op jit(solution)/shard_map/dot_general | solution.py:54
  100.1 0.0 copy-done.3
  100.1 0.0 copy-done.5
  100.1 7.4 %multiply_convert_fusion = bf16[2560,2560]{1,0:T(8,128)(2,1)} fusion(f32[]{:T(128)} %fusion.51, bf16[1,256,2560]{2,1,0:T(8,128)(2,1)S(1)} %copy-done.3, bf16[1,256,2560]{2,1,0:T(8,128)(2,1)S(1)} %copy-done.5, f32[256]{0:T(256)S(1)} %add_rsqrt_fusion, f32[2560]{0:T(1024)S(1)} %reduce.1), kind=kOutput, calls=%fused_computation.2 | convolution fusion | flops 3371171840 | bytes 15739908 | tf_op jit(solution)/shard_map/dot_general | solution.py:70
  107.5 0.0 copy-start.6
  107.5 0.0 copy-start
  107.5 0.0 reduce-scatter.2.cloned.1.call-update
  107.5 0.6 copy-done.6
  108.1 0.2 convert_reduce_fusion.1
  108.3 0.5 copy-done
  108.8 0.3 fusion.17
  109.2 8.3 %fusion.10 = bf16[256,2560]{1,0:T(8,128)(2,1)S(1)} fusion(bf16[1,2560,2560]{2,1,0:T(8,128)(2,1)} %all-gather.2.cloned.1.call-done, bf16[1,256,2560]{2,1,0:T(8,128)(2,1)S(1)} %copy-done, f32[2560]{0:T(1024)S(1)} %reduce.1, f32[256]{0:T(256)S(1)} %add_rsqrt_fusion.1), kind=kOutput, calls=%fused_computation.9 | convolution fusion | flops 3360030720 | bytes 15739904 | tf_op jit(solution)/shard_map/dot_general | solution.py:53
  117.5 0.6 reshape.253
  118.1 0.5 convolution_convert_fusion.1
  118.6 1.5 copy.11
  120.1 0.0 copy-start.7
  120.1 0.0 copy-start.4
  120.1 5.5 %all-to-all-start = ((bf16[16,16,2560]{2,1,0:T(8,128)(2,1)}), bf16[16,16,2560]{2,1,0:T(8,128)(2,1)}, u32[]{:S(2)}, u32[]{:S(2)}) async-start(bf16[16,16,2560]{2,1,0:T(8,128)(2,1)} %bitcast.15), calls=%async_computation | async-start | bytes 2621440 | tf_op jit(solution)/shard_map/all_to_all | solution.py:80
  125.6 0.0 copy-done.7
  125.6 0.2 convert_reduce_fusion
  125.8 0.0 copy-done.4
  125.8 3.3 fusion.25
  129.0 0.6 reshape.256
  129.7 0.5 convolution_convert_fusion
  130.2 1.5 copy.12
  131.6 0.0 copy-start.8
  131.6 23.6 %all-to-all-done = bf16[16,16,2560]{2,1,0:T(8,128)(2,1)} async-done(((bf16[16,16,2560]{2,1,0:T(8,128)(2,1)}), bf16[16,16,2560]{2,1,0:T(8,128)(2,1)}, u32[]{:S(2)}, u32[]{:S(2)}) %all-to-all-start) | async-done | bytes 1310752 | tf_op jit(solution)/shard_map/all_to_all | solution.py:80
  155.2 7.7 %all-to-all-start.1 = ((bf16[16,16,2560]{2,1,0:T(8,128)(2,1)}), bf16[16,16,2560]{2,1,0:T(8,128)(2,1)S(1)}, u32[]{:S(2)}, u32[]{:S(2)}) async-start(bf16[16,16,2560]{2,1,0:T(8,128)(2,1)} %bitcast.17), calls=%async_computation.1 | async-start | bytes 2621440 | tf_op jit(solution)/shard_map/all_to_all | solution.py:81
  162.9 4.2 %collective-permute-start = (bf16[16,16,2560]{2,1,0:T(8,128)(2,1)}, bf16[16,16,2560]{2,1,0:T(8,128)(2,1)S(1)}, u32[]{:S(2)}, u32[]{:S(2)}) collective-permute-start(bf16[16,16,2560]{2,1,0:T(8,128)(2,1)} %all-to-all-done), channel_id=1, source_target_pairs={{0,16},{16,32},{32,48},{48,64},{64,80},{80,96},{96,112},{112,128},... | collective-permute-start | bytes 3932168 | tf_op jit(solution)/shard_map/ppermute | solution.py:12
  167.1 53.7 %all-to-all-done.1 = bf16[16,16,2560]{2,1,0:T(8,128)(2,1)S(1)} async-done(((bf16[16,16,2560]{2,1,0:T(8,128)(2,1)}), bf16[16,16,2560]{2,1,0:T(8,128)(2,1)S(1)}, u32[]{:S(2)}, u32[]{:S(2)}) %all-to-all-start.1) | async-done | bytes 1310752 | tf_op jit(solution)/shard_map/all_to_all | solution.py:81
  220.8 4.9 %collective-permute-start.1 = (bf16[16,16,2560]{2,1,0:T(8,128)(2,1)S(1)}, bf16[16,16,2560]{2,1,0:T(8,128)(2,1)S(1)}, u32[]{:S(2)}, u32[]{:S(2)}) collective-permute-start(bf16[16,16,2560]{2,1,0:T(8,128)(2,1)S(1)} %all-to-all-done.1), channel_id=1, source_target_pairs={{16,0},{32,16},{48,32},{64,48},{80,64},{96,80},{112,96},{128,112},... | collective-permute-start | bytes 3932168 | tf_op jit(solution)/shard_map/ppermute | solution.py:12
  225.7 0.0 copy-done.8
  225.7 0.6 fusion.52
  226.3 0.0 collective-permute-done
  226.3 81.7 %collective-permute-done.1 = bf16[16,16,2560]{2,1,0:T(8,128)(2,1)S(1)} collective-permute-done((bf16[16,16,2560]{2,1,0:T(8,128)(2,1)S(1)}, bf16[16,16,2560]{2,1,0:T(8,128)(2,1)S(1)}, u32[]{:S(2)}, u32[]{:S(2)}) %collective-permute-start.1) | collective-permute-done | bytes 1310752 | tf_op jit(solution)/shard_map/ppermute | solution.py:12
  308.0 0.0 copy-start.1
  308.0 1.1 copy-done.1
  309.1 51.0 %reduce-scatter.2.cloned.1.call-done = bf16[160,2560]{1,0:T(8,128)(2,1)} async-done(((bf16[2560,2560]{1,0:T(8,128)(2,1)}), bf16[160,2560]{1,0:T(8,128)(2,1)}) %reduce-scatter.2.cloned.1.call-update) | async-done | bytes 819216 | tf_op jit(solution)/shard_map/reduce_scatter | solution.py:73
  360.1 3.1 divide_bitcast_fusion
  363.2 0.0 copy-start.2
  363.2 1.1 copy.15
  364.3 0.7 copy-done.2
  365.0 1.1 copy.16
  (5 shorter events, 0.0 us)
Async XLA Ops:
  7.2 82.4 %all-gather.2.cloned.1.call-start = ((), (), s32[]{:S(2)}) async-start(), calls=%async_computation.3 | async-start | bytes 13926400 | tf_op jit(solution)/shard_map/all_gather | solution.py:51
  7.9 352.2 %reduce-scatter.2.cloned.1.call-start = ((), (), s32[]{:S(2)}) async-start(), calls=%async_computation.4 | async-start | bytes 13926400 | tf_op jit(solution)/shard_map/reduce_scatter | solution.py:73
  10.0 90.2 %copy-start.3 = (bf16[1,256,2560]{2,1,0:T(8,128)(2,1)S(1)}, bf16[1,256,2560]{2,1,0:T(8,128)(2,1)}, u32[]{:S(2)}) copy-start(bf16[1,256,2560]{2,1,0:T(8,128)(2,1)} %param.9) | copy-start | bytes 3932164
  10.0 90.2 %copy-start.5 = (bf16[1,256,2560]{2,1,0:T(8,128)(2,1)S(1)}, bf16[1,256,2560]{2,1,0:T(8,128)(2,1)}, u32[]{:S(2)}) copy-start(bf16[1,256,2560]{2,1,0:T(8,128)(2,1)} %param.10) | copy-start | bytes 3932164
  107.5 0.7 copy-start.6
  107.5 1.3 copy-start
  120.1 5.5 %copy-start.7 = (s32[1,16,1]{1,2,0:T(1,128)S(1)}, s32[1,16,1]{1,2,0:T(1,128)}, u32[]{:S(2)}) copy-start(s32[1,16,1]{1,2,0:T(1,128)} %param.14) | copy-start | bytes 196
  120.1 5.7 %copy-start.4 = (bf16[1,256,2560]{2,1,0:T(8,128)(2,1)S(1)}, bf16[1,256,2560]{2,1,0:T(8,128)(2,1)}, u32[]{:S(2)}) copy-start(bf16[1,256,2560]{2,1,0:T(8,128)(2,1)} %param.9) | copy-start | bytes 3932164
  120.1 35.1 %all-to-all-start = ((bf16[16,16,2560]{2,1,0:T(8,128)(2,1)}), bf16[16,16,2560]{2,1,0:T(8,128)(2,1)}, u32[]{:S(2)}, u32[]{:S(2)}) async-start(bf16[16,16,2560]{2,1,0:T(8,128)(2,1)} %bitcast.15), calls=%async_computation | async-start | bytes 2621440 | tf_op jit(solution)/shard_map/all_to_all | solution.py:80
  131.6 94.1 %copy-start.8 = (s32[1,16]{1,0:T(1,128)S(1)}, s32[1,16]{1,0:T(1,128)}, u32[]{:S(2)}) copy-start(s32[1,16]{1,0:T(1,128)} %param.15) | copy-start | bytes 196
  155.2 65.6 %all-to-all-start.1 = ((bf16[16,16,2560]{2,1,0:T(8,128)(2,1)}), bf16[16,16,2560]{2,1,0:T(8,128)(2,1)S(1)}, u32[]{:S(2)}, u32[]{:S(2)}) async-start(bf16[16,16,2560]{2,1,0:T(8,128)(2,1)} %bitcast.17), calls=%async_computation.1 | async-start | bytes 2621440 | tf_op jit(solution)/shard_map/all_to_all | solution.py:81
  162.9 63.4 %collective-permute-start = (bf16[16,16,2560]{2,1,0:T(8,128)(2,1)}, bf16[16,16,2560]{2,1,0:T(8,128)(2,1)S(1)}, u32[]{:S(2)}, u32[]{:S(2)}) collective-permute-start(bf16[16,16,2560]{2,1,0:T(8,128)(2,1)} %all-to-all-done), channel_id=1, source_target_pairs={{0,16},{16,32},{32,48},{48,64},{64,80},{80,96},{96,112},{112,128},... | collective-permute-start | bytes 3932168 | tf_op jit(solution)/shard_map/ppermute | solution.py:12
  220.8 87.2 %collective-permute-start.1 = (bf16[16,16,2560]{2,1,0:T(8,128)(2,1)S(1)}, bf16[16,16,2560]{2,1,0:T(8,128)(2,1)S(1)}, u32[]{:S(2)}, u32[]{:S(2)}) collective-permute-start(bf16[16,16,2560]{2,1,0:T(8,128)(2,1)S(1)} %all-to-all-done.1), channel_id=1, source_target_pairs={{16,0},{32,16},{48,32},{64,48},{80,64},{96,80},{112,96},{128,112},... | collective-permute-start | bytes 3932168 | tf_op jit(solution)/shard_map/ppermute | solution.py:12
  308.0 1.1 copy-start.1
  363.2 1.8 copy-start.2
Sparse Core Ops, SparseCore 0:
  9.8 79.6 all-gather.1
  107.6 252.3 reduce-scatter.1
where the time goes:
time: 378 us; the launch traced here: 373 us
  waiting for transfers between devices  290 us (77%)
  matrix products  27.2 us (7%)
  starting transfers between devices  22.2 us (6%)
  between operations  14.2 us (4%)
  other arithmetic  9.73 us (3%)
  local copies, waits for them, and re-layouts  9.24 us (2%)
    ppermute x2, waiting for transfers between devices, shifted(): return lax.ppermute(x, axis, pairs)  81.7 us
    all_gather x1, waiting for transfers between devices, local(): piece_rows = lax.all_gather(proj, 'peer', axis=1, tiled=True)[0]  79.6 us
    all_to_all x1, waiting for transfers between devices, local(): lax.all_to_all(send_down, 'peer', split_axis=0, concat_axis=0, tiled=True)  53.7 us
    reduce_scatter x1, waiting for transfers between devices, local(): lax.psum_scatter((keep_mine * product).astype(jnp.bfloat16), 'peer', scat...  51 us
    all_to_all x1, waiting for transfers between devices, local(): lax.all_to_all(send_up, 'peer', split_axis=0, concat_axis=0, tiled=True)  23.6 us
    dot_general x1, matrix products, local(): lax.dot_general(cot_b, piece_rows, (((1,), (1,)), ((), ())), preferred_el...  10.5 us
    ppermute x2, starting transfers between devices, shifted(): return lax.ppermute(x, axis, pairs)  9.04 us
    dot_general x1, matrix products, local(): jnp.dot(columns, piece_rows, preferred_element_type=jnp.float32)  8.31 us
  transfers between devices with their start and end apart: 6, of which 5 were waited for; matrix products, arithmetic and copies ran while one was open for 5% of the time, Pallas kernels for 0%

commit v1 on v0

v1 whole, which is shorter than its diff:
```python
import jax
import jax.numpy as jnp
from jax import lax
from jax.experimental import pallas as pl
from jax.experimental.pallas import tpu as pltpu
from jax.sharding import PartitionSpec as P

MESH = pl.DeviceIdType.MESH
F32 = jnp.float32
BF16 = jnp.bfloat16
EPS = 1e-05

SECTIONS = 16
PEERS = 16
C = 2560
TOK = 256
BLK = 16
SH = C // PEERS
HALF = SH // 2
GRP = 4 * SH
TILE = 512


def dot(a, b, dims):
    return lax.dot_general(a, b, (dims, ((), ())), preferred_element_type=F32)


def kernel(
    acts_f, acts_b, cot, gain, proj, froute, broute, strag,
    next_o, back_o, dw_o,
    wg, af, ab, aperm, bperm, cperm, na, nb, nbt, nbq, cotq, hacc, gn, ostage, gstage,
    psend, rs_half, rs_full,
    loc_sem, ag_ss, ag_rs, sib_ss, sib_rs, ex_ss, ex_rs, nb_ss, nb_rs, red_ss, red_rs, a2a_ss, a2a_rs,
):
    s = lax.axis_index("section")
    q = lax.axis_index("peer")
    x = lax.div(q, 4)
    quad = lax.rem(q, 4)
    z = lax.div(quad, 2)
    c = lax.rem(q, 2)
    xr = lax.rem(x + 1, 4)
    xl = lax.rem(x + 3, 4)
    x2 = lax.rem(x + 2, 4)
    up = lax.rem(s + 1, SECTIONS)
    down = lax.rem(s + SECTIONS - 1, SECTIONS)

    def peer(px, pz, pc):
        return px * 4 + pz * 2 + pc

    right = (s, peer(xr, z, c))
    left = (s, peer(xl, z, c))
    zpart = (s, peer(x, 1 - z, c))
    sib = (s, peer(x, z, 1 - c))
    diag = (s, peer(x, 1 - z, 1 - c))

    bar = pltpu.get_barrier_semaphore()
    for dev in (right, left, zpart, sib, diag):
        pl.semaphore_signal(bar, inc=1, device_id=dev, device_id_type=MESH)

    def greet(i, carry):
        pl.semaphore_signal(bar, inc=1, device_id=(up, i), device_id_type=MESH)
        pl.semaphore_signal(bar, inc=1, device_id=(down, i), device_id_type=MESH)
        return carry

    lax.fori_loop(0, PEERS, greet, 0)
    pl.semaphore_wait(bar, 5 + 2 * PEERS)

    def remote(src, dst, ss, rs, dev):
        return pltpu.make_async_remote_copy(
            src_ref=src, dst_ref=dst, send_sem=ss, recv_sem=rs, device_id=dev, device_id_type=MESH
        )

    def rows(px, pz, lo=0, n=SH, pc=c):
        return wg.at[pl.ds(pl.multiple_of(peer(px, pz, pc) * SH + lo, 16), n)]

    sent = []

    def send(src, dst, ss, rs, dev):
        cp = remote(src, dst, ss, rs, dev)
        cp.start()
        sent.append(cp)

    def ag_send(src, region, k_send, k_recv, dev):
        send(src, region, ag_ss.at[k_send], ag_rs.at[k_recv], dev)

    def ag_wait(region, k_recv):
        remote(region, region, ag_ss.at[0], ag_rs.at[k_recv], zpart).wait_recv()

    def sib_send(src, region, k):
        send(src, region, sib_ss.at[k], sib_rs.at[k], sib)

    def sib_wait(px, pz, k, lo=0, n=SH):
        region = rows(px, pz, lo, n, 1 - c)
        remote(region, region, sib_ss.at[k], sib_rs.at[k], sib).wait_recv()

    ag_send(proj, rows(x, z), 0, 0, zpart)
    ag_send(proj, rows(x, z), 1, 1, right)
    ag_send(proj, rows(x, z), 2, 5, left)
    sib_send(proj, rows(x, z), 0)
    own_slot = pl.ds(pl.multiple_of(quad * TOK, TOK), TOK)
    loads = [
        pltpu.make_async_copy(acts_b, ab, loc_sem.at[0]),
        pltpu.make_async_copy(acts_f, af, loc_sem.at[1]),
        pltpu.make_async_copy(cot, cotq.at[own_slot], loc_sem.at[2]),
        pltpu.make_async_copy(proj, rows(x, z), loc_sem.at[3]),
    ]
    for cp in loads:
        cp.start()
    send(cot, cotq.at[own_slot], ex_ss.at[0], ex_rs.at[0], sib)

    count = jnp.float32(0)
    for i in range(PEERS):
        count = count + (1 - strag[0, i]).astype(F32)
    keep = (1 - strag[0, q]).astype(F32)

    loads[0].wait()

    def norm_b(i, carry):
        r = pl.ds(pl.multiple_of(i * 16, 16), 16)
        wide = ab[r].astype(F32)
        rstd = lax.rsqrt(jnp.mean(wide * wide, axis=-1, keepdims=True) + EPS)
        nb[r] = (wide * rstd * gain[...] * keep).astype(BF16)
        return carry

    lax.fori_loop(0, TOK // 16, norm_b, 0)

    def turn(i, carry):
        cols = pl.ds(pl.multiple_of(i * GRP, GRP), GRP)
        t = nb[:, cols].T
        for k in range(4):
            nbt[k, pl.ds(pl.multiple_of(i * SH, SH), SH)] = t[k * SH:(k + 1) * SH]
        return carry

    lax.fori_loop(0, 4, turn, 0)
    nb_sib = peer(0, z, 1 - c)
    nb_z = peer(0, 1 - z, c)
    nb_diag = peer(0, 1 - z, 1 - c)
    send(nbt.at[nb_sib], nbq.at[quad], nb_ss.at[0], nb_rs.at[0], sib)
    nbq[quad] = nbt[quad]

    def ordering(route_ref):
        st = (route_ref[...] == lax.broadcasted_iota(jnp.int32, (PEERS, PEERS), 1)).astype(F32).astype(BF16)
        e = ((lax.broadcasted_iota(jnp.int32, (TOK, PEERS), 0) >> 4)
             == lax.broadcasted_iota(jnp.int32, (TOK, PEERS), 1)).astype(F32).astype(BF16)
        er = dot(e, st, ((1,), (1,))).astype(BF16)
        full = dot(er, e, ((1,), (1,)))
        same = (lax.broadcasted_iota(jnp.int32, (TOK, TOK), 0) & 15) == (
            lax.broadcasted_iota(jnp.int32, (TOK, TOK), 1) & 15)
        return jnp.where(same, full, 0.0).astype(BF16)

    def reorder(order, src, dst):
        def body(i, carry):
            cols = pl.ds(pl.multiple_of(i * TILE, TILE), TILE)
            dst[:, cols] = dot(order, src[:, cols], ((1,), (0,))).astype(BF16)
            return carry

        lax.fori_loop(0, C // TILE, body, 0)

    loads[1].wait()
    reorder(ordering(froute), af, aperm)

    def norm_a(i, carry):
        r = pl.ds(pl.multiple_of(i * 16, 16), 16)
        wide = aperm[r].astype(F32)
        rstd = lax.rsqrt(jnp.mean(wide * wide, axis=-1, keepdims=True) + EPS)
        na[r] = (wide * rstd * gain[...]).astype(BF16)
        return carry

    lax.fori_loop(0, TOK // 16, norm_a, 0)
    order_b = ordering(broute)
    reorder(order_b, ab, bperm)
    loads[2].wait()
    reorder(order_b, cotq.at[own_slot], cperm)
    loads[3].wait()

    ag_wait(rows(x, 1 - z), 0)
    ag_send(rows(x, 1 - z), rows(x, 1 - z), 3, 2, right)
    ag_send(rows(x, 1 - z), rows(x, 1 - z), 4, 6, left)
    sib_send(rows(x, 1 - z), rows(x, 1 - z), 1)
    send(cot, cotq.at[own_slot], ex_ss.at[1], ex_rs.at[1], zpart)
    send(nbt.at[nb_z], nbq.at[quad], nb_ss.at[1], nb_rs.at[1], zpart)
    send(nbt.at[nb_diag], nbq.at[quad], nb_ss.at[2], nb_rs.at[2], diag)

    ag_wait(rows(xl, z), 1)
    ag_send(rows(xl, z, 0, HALF), rows(xl, z, 0, HALF), 5, 3, right)
    sib_send(rows(xl, z), rows(xl, z), 2)
    ag_wait(rows(xr, z), 5)
    ag_send(rows(xr, z, HALF, HALF), rows(xr, z, HALF, HALF), 6, 7, left)
    sib_send(rows(xr, z), rows(xr, z), 3)

    def base_of(px):
        return pl.multiple_of(px * GRP, GRP)

    def hidden_group(px, first, last):
        base = base_of(px)

        def body(i, carry):
            cols = pl.ds(pl.multiple_of(i * TILE, TILE), TILE)
            part = dot(na[:, pl.ds(base, GRP)], wg[pl.ds(base, GRP), cols], ((1,), (0,)))
            if not first:
                part = part + hacc[:, cols]
            if last:
                ostage[:, cols] = (aperm[:, cols].astype(F32) + part).astype(BF16)
            else:
                hacc[:, cols] = part
            return carry

        lax.fori_loop(0, C // TILE, body, 0)

    def grad_group(px):
        base = base_of(px)

        def body(i, carry):
            at = pl.multiple_of(base + i * 128, 128)
            gn[:, pl.ds(at, 128)] = dot(cperm[...], wg[pl.ds(at, 128)], ((1,), (1,)))
            return carry

        lax.fori_loop(0, GRP // 128, body, 0)

    sib_wait(x, z, 0)
    sib_wait(x, 1 - z, 1)
    hidden_group(x, True, False)
    grad_group(x)

    ag_wait(rows(xl, 1 - z), 2)
    ag_send(rows(xl, 1 - z, 0, HALF), rows(xl, 1 - z, 0, HALF), 7, 4, right)
    sib_send(rows(xl, 1 - z), rows(xl, 1 - z), 4)
    ag_wait(rows(xr, 1 - z), 6)
    ag_send(rows(xr, 1 - z, HALF, HALF), rows(xr, 1 - z, HALF, HALF), 8, 8, left)
    sib_send(rows(xr, 1 - z), rows(xr, 1 - z), 5)

    sib_wait(xl, z, 2)
    sib_wait(xl, 1 - z, 4)
    hidden_group(xl, False, False)
    grad_group(xl)
    sib_wait(xr, z, 3)
    sib_wait(xr, 1 - z, 5)
    hidden_group(xr, False, False)
    grad_group(xr)

    ag_wait(rows(x2, z, 0, HALF), 3)
    sib_send(rows(x2, z, 0, HALF), rows(x2, z, 0, HALF), 6)
    ag_wait(rows(x2, z, HALF, HALF), 7)
    sib_send(rows(x2, z, HALF, HALF), rows(x2, z, HALF, HALF), 7)
    ag_wait(rows(x2, 1 - z, 0, HALF), 4)
    sib_send(rows(x2, 1 - z, 0, HALF), rows(x2, 1 - z, 0, HALF), 8)
    ag_wait(rows(x2, 1 - z, HALF, HALF), 8)
    sib_send(rows(x2, 1 - z, HALF, HALF), rows(x2, 1 - z, HALF, HALF), 9)
    sib_wait(x2, z, 6, 0, HALF)
    sib_wait(x2, z, 7, HALF, HALF)
    sib_wait(x2, 1 - z, 8, 0, HALF)
    sib_wait(x2, 1 - z, 9, HALF, HALF)

    hidden_group(x2, False, True)

    def deal(stage, out, k, section):
        def body(i, carry):
            p = lax.rem(q + i, PEERS)
            remote(
                stage.at[pl.ds(pl.multiple_of(p * BLK, BLK), BLK)],
                out.at[pl.ds(pl.multiple_of(q * BLK, BLK), BLK)],
                a2a_ss.at[k], a2a_rs.at[k], (section, p),
            ).start()
            return carry

        lax.fori_loop(0, PEERS, body, 0)

    @pl.when(s < SECTIONS - 1)
    def _():
        deal(ostage, next_o, 0, up)

    grad_group(x2)

    def grad_rows(i, carry):
        r = pl.ds(pl.multiple_of(i * 16, 16), 16)
        wide = bperm[r].astype(F32)
        rstd = lax.rsqrt(jnp.mean(wide * wide, axis=-1, keepdims=True) + EPS)
        scaled = gain[...] * gn[r]
        inner = jnp.mean(wide * scaled, axis=-1, keepdims=True)
        gstage[r] = (cperm[r].astype(F32) + rstd * scaled - wide * (rstd * rstd * rstd * inner)).astype(BF16)
        return carry

    lax.fori_loop(0, TOK // 16, grad_rows, 0)

    @pl.when(s > 0)
    def _():
        deal(gstage, back_o, 1, down)

    def slot(pz, pc):
        return cotq.at[pl.ds(pl.multiple_of(peer(0, pz, pc) * TOK, TOK), TOK)]

    def ex_wait(region, k):
        remote(region, region, ex_ss.at[0], ex_rs.at[k], sib).wait_recv()

    ex_wait(slot(1 - z, c), 1)
    send(slot(1 - z, c), slot(1 - z, c), ex_ss.at[2], ex_rs.at[2], sib)
    ex_wait(slot(z, 1 - c), 0)
    for k, src in enumerate((nb_sib, nb_z, nb_diag)):
        remote(nbq.at[src], nbq.at[src], nb_ss.at[0], nb_rs.at[k], sib).wait_recv()
    ex_wait(slot(1 - z, 1 - c), 2)

    def partial(px, cols):
        r = pl.ds(pl.multiple_of(px * SH, SH), SH)
        acc = dot(nbq[0, r], cotq[pl.ds(0, TOK), cols], ((1,), (0,)))
        for k in range(1, 4):
            acc = acc + dot(nbq[k, r], cotq[pl.ds(k * TOK, TOK), cols], ((1,), (0,)))
        return acc

    def partial_to(px, k):
        def body(i, carry):
            cols = pl.ds(pl.multiple_of(i * TILE, TILE), TILE)
            psend[k, :, cols] = partial(px, cols).astype(BF16)
            return carry

        lax.fori_loop(0, C // TILE, body, 0)

    first = pl.ds(0, HALF)
    second = pl.ds(HALF, HALF)
    partial_to(x2, 0)
    send(psend.at[0, first], rs_half.at[0], red_ss.at[0], red_rs.at[0], right)
    send(psend.at[0, second], rs_half.at[1], red_ss.at[1], red_rs.at[1], left)
    partial_to(xr, 1)
    send(psend.at[1, second], rs_full.at[0, second], red_ss.at[2], red_rs.at[3], right)
    partial_to(xl, 2)
    send(psend.at[2, first], rs_full.at[1, first], red_ss.at[3], red_rs.at[4], left)

    def own(i, carry):
        cols = pl.ds(pl.multiple_of(i * TILE, TILE), TILE)
        dw_o[:, cols] = partial(x, cols)
        return carry

    lax.fori_loop(0, C // TILE, own, 0)

    def add_half(k, half, region):
        def body(i, carry):
            r = pl.ds(pl.multiple_of(i * 16, 16), 16)
            at = pl.ds(pl.multiple_of(half * HALF + i * 16, 16), 16)
            psend[k, at] = (psend[k, at].astype(F32) + rs_half[half, r].astype(F32)).astype(BF16)
            return carry

        lax.fori_loop(0, HALF // 16, body, 0)

    remote(rs_half.at[0], rs_half.at[0], red_ss.at[0], red_rs.at[0], left).wait_recv()
    add_half(1, 0, first)
    send(psend.at[1, first], rs_full.at[0, first], red_ss.at[4], red_rs.at[2], right)
    remote(rs_half.at[1], rs_half.at[1], red_ss.at[0], red_rs.at[1], right).wait_recv()
    add_half(2, 1, second)
    send(psend.at[2, second], rs_full.at[1, second], red_ss.at[5], red_rs.at[5], left)

    for side in range(2):
        for h, part in enumerate((first, second)):
            region = rs_full.at[side, part]
            remote(region, region, red_ss.at[0], red_rs.at[2 + 2 * side + h], left).wait_recv()

    def finish(i, carry):
        r = pl.ds(pl.multiple_of(i * 16, 16), 16)
        dw_o[r] = (dw_o[r] + rs_full[0, r].astype(F32) + rs_full[1, r].astype(F32)) / count
        return carry

    lax.fori_loop(0, SH // 16, finish, 0)

    for cp in sent:
        cp.wait_send()

    @pl.when(s < SECTIONS - 1)
    def _():
        remote(ostage, next_o, a2a_ss.at[0], a2a_rs.at[0], sib).wait_send()

    @pl.when(s > 0)
    def _():
        remote(gstage, back_o, a2a_ss.at[1], a2a_rs.at[1], sib).wait_send()

    @pl.when(s > 0)
    def _():
        remote(ostage, next_o, a2a_ss.at[0], a2a_rs.at[0], sib).wait_recv()

    @pl.when(s < SECTIONS - 1)
    def _():
        remote(gstage, back_o, a2a_ss.at[1], a2a_rs.at[1], sib).wait_recv()

    @pl.when(s == 0)
    def _():
        nb[...] = jnp.zeros_like(nb)
        cp = pltpu.make_async_copy(nb, next_o, loc_sem.at[0])
        cp.start()
        cp.wait()

    @pl.when(s == SECTIONS - 1)
    def _():
        nb[...] = jnp.zeros_like(nb)
        cp = pltpu.make_async_copy(nb, back_o, loc_sem.at[0])
        cp.start()
        cp.wait()


def local(acts_fwd, acts_bwd, cot_bwd, gain, proj, fwd_route, bwd_route, straggler):
    hbm = pl.BlockSpec(memory_space=pl.ANY)
    vmem = pl.BlockSpec(memory_space=pltpu.VMEM)
    smem = pl.BlockSpec(memory_space=pltpu.SMEM)
    dma = pltpu.SemaphoreType.DMA
    out = pl.pallas_call(
        kernel,
        name="swarm_tick",
        out_shape=(
            jax.ShapeDtypeStruct((TOK, C), BF16),
            jax.ShapeDtypeStruct((TOK, C), BF16),
            jax.ShapeDtypeStruct((SH, C), F32),
        ),
        in_specs=[hbm, hbm, hbm, vmem, hbm, vmem, vmem, smem],
        out_specs=(hbm, hbm, vmem),
        scratch_shapes=[
            pltpu.VMEM((C, C), BF16),
            pltpu.VMEM((TOK, C), BF16),
            pltpu.VMEM((TOK, C), BF16),
            pltpu.VMEM((TOK, C), BF16),
            pltpu.VMEM((TOK, C), BF16),
            pltpu.VMEM((TOK, C), BF16),
            pltpu.VMEM((TOK, C), BF16),
            pltpu.VMEM((TOK, C), BF16),
            pltpu.VMEM((4, GRP, TOK), BF16),
            pltpu.VMEM((4, GRP, TOK), BF16),
            pltpu.VMEM((4 * TOK, C), BF16),
            pltpu.VMEM((TOK, C), F32),
            pltpu.VMEM((TOK, C), F32),
            pltpu.VMEM((TOK, C), BF16),
            pltpu.VMEM((TOK, C), BF16),
            pltpu.VMEM((3, SH, C), BF16),
            pltpu.VMEM((2, HALF, C), BF16),
            pltpu.VMEM((2, SH, C), BF16),
            dma((4,)),
            dma((9,)), dma((9,)),
            dma((10,)), dma((10,)),
            dma((3,)), dma((3,)),
            dma((3,)), dma((3,)),
            dma((6,)), dma((6,)),
            dma((2,)), dma((2,)),
        ],
        compiler_params=pltpu.CompilerParams(
            collective_id=0, has_side_effects=True, vmem_limit_bytes=56 * 2**20
        ),
        cost_estimate=pl.CostEstimate(
            flops=6 * TOK * C * C, bytes_accessed=20 * 2**20, transcendentals=0
        ),
    )(
        acts_fwd[0], acts_bwd[0], cot_bwd[0], gain, proj[0], fwd_route[0], bwd_route[0], straggler
    )
    return tuple(o[None] for o in out)


def solution(mesh):
    split = P("section", "peer", None)
    whole = P("section", None)
    return jax.shard_map(
        local,
        mesh=mesh,
        in_specs=(split, split, split, whole, split, split, split, whole),
        out_specs=(split, split, split),
        check_vma=False,
    )
```

time: 378 us -> 151 us (0.40)
  the two profiles are of different devices: /device:TPU:49 before, /device:TPU:39 now
where the time goes in v1:
time: 151 us
  Pallas kernels  142 us (94%)
  local copies, waits for them, and re-layouts  8.29 us (5%)
    pallas_call x1, Pallas kernels, local(): pl.pallas_call(kernel, name='swarm_tick', out_shape=(jax.ShapeDtypeStruct...  142 us
    unnamed x7, local copies, waits for them, and re-layouts  5.63 us

profile of v1, /device:TPU:39, one launch (start us, length us, event | category | flops | bytes accessed | tf_op | source)
XLA Modules:
  0.0 151.2 jit_solution(17572399771478341557)
XLA Ops:
  0.6 1.3 copy.11.froute
  2.0 1.3 copy.12.broute
  3.3 142.3 %swarm_tick.1 = (bf16[256,2560]{1,0:T(8,128)(2,1)}, bf16[256,2560]{1,0:T(8,128)(2,1)}, f32[160,2560]{1,0:T(8,128)}) custom-call(bf16[256,2560]{1,0:T(8,128)(2,1)} %bitcast.14, bf16[256,2560]{1,0:T(8,128)(2,1)} %bitcast.15, bf16[256,2560]{1,0:T(8,128)(2,1)} %bitcast.16, f32[1,2560]{1,0:T(1,128)} %gain.1, bf16[160,2560]{1,0:T(8,128)(2,1)} %bitcast.17, ...), custom_call_target="tpu_custom_call" | custom-call | flops 10066329600 | bytes 20971520 | tf_op jit(solution)/shard_map/swarm_tick/pallas_call | solution.py:401
  145.6 0.0 copy-start.1
  145.6 2.6 %copy.16 = bf16[1,256,2560]{2,1,0:T(8,128)(2,1)} copy(bf16[1,256,2560]{2,1,0:T(8,128)(2,1)} %bitcast.11) | data formatting | bytes 2621440
  148.2 0.0 copy-done.1
  148.2 0.0 copy-start
  148.2 1.1 copy.17
  149.2 0.8 copy-done
  150.1 1.2 copy.18
Async XLA Ops:
  145.6 2.6 %copy-start.1 = (bf16[256,2560]{1,0:T(8,128)(2,1)S(1)}, bf16[256,2560]{1,0:T(8,128)(2,1)}, u32[]{:S(2)}) copy-start(bf16[256,2560]{1,0:T(8,128)(2,1)} %get-tuple-element.7) | copy-start | bytes 3932164
  148.2 1.9 %copy-start = (f32[160,2560]{1,0:T(8,128)S(1)}, f32[160,2560]{1,0:T(8,128)}, u32[]{:S(2)}) copy-start(f32[160,2560]{1,0:T(8,128)} %get-tuple-element.8) | copy-start | bytes 4915204

commit v2 on v1

--- a/solution.py
+++ b/solution.py
@@ -9,6 +9,8 @@
 F32 = jnp.float32
 BF16 = jnp.bfloat16
 EPS = 1e-05
+START = 7
+STRIDE = 1
 
 SECTIONS = 16
 PEERS = 16
@@ -30,7 +32,7 @@
     next_o, back_o, dw_o,
     wg, af, ab, aperm, bperm, cperm, na, nb, nbt, nbq, cotq, hacc, gn, ostage, gstage,
     psend, rs_half, rs_full,
-    loc_sem, ag_ss, ag_rs, sib_ss, sib_rs, ex_ss, ex_rs, nb_ss, nb_rs, red_ss, red_rs, a2a_ss, a2a_rs,
+    loc_sem, ag_ss, ag_rs, sib_ss, sib_rs, ex_ss, ex_rs, nb_ss, nb_rs, red_ss, red_rs, a2a_ss, a2a_rs, ready,
 ):
     s = lax.axis_index("section")
     q = lax.axis_index("peer")
@@ -54,16 +56,9 @@
     diag = (s, peer(x, 1 - z, 1 - c))
 
     bar = pltpu.get_barrier_semaphore()
-    for dev in (right, left, zpart, sib, diag):
+    for dev in (right, left, zpart, sib, diag, (up, q), (down, q)):
         pl.semaphore_signal(bar, inc=1, device_id=dev, device_id_type=MESH)
-
-    def greet(i, carry):
-        pl.semaphore_signal(bar, inc=1, device_id=(up, i), device_id_type=MESH)
-        pl.semaphore_signal(bar, inc=1, device_id=(down, i), device_id_type=MESH)
-        return carry
-
-    lax.fori_loop(0, PEERS, greet, 0)
-    pl.semaphore_wait(bar, 5 + 2 * PEERS)
+    pl.semaphore_wait(bar, 7)
 
     def remote(src, dst, ss, rs, dev):
         return pltpu.make_async_remote_copy(
@@ -139,10 +134,10 @@
     nbq[quad] = nbt[quad]
 
     def ordering(route_ref):
-        st = (route_ref[...] == lax.broadcasted_iota(jnp.int32, (PEERS, PEERS), 1)).astype(F32).astype(BF16)
+        st = (route_ref[...] == lax.broadcasted_iota(jnp.int32, (PEERS, PEERS), 0)).astype(F32).astype(BF16)
         e = ((lax.broadcasted_iota(jnp.int32, (TOK, PEERS), 0) >> 4)
              == lax.broadcasted_iota(jnp.int32, (TOK, PEERS), 1)).astype(F32).astype(BF16)
-        er = dot(e, st, ((1,), (1,))).astype(BF16)
+        er = dot(e, st, ((1,), (0,))).astype(BF16)
         full = dot(er, e, ((1,), (1,)))
         same = (lax.broadcasted_iota(jnp.int32, (TOK, TOK), 0) & 15) == (
             lax.broadcasted_iota(jnp.int32, (TOK, TOK), 1) & 15)
@@ -172,6 +167,20 @@
     loads[2].wait()
     reorder(order_b, cotq.at[own_slot], cperm)
     loads[3].wait()
+
+    @pl.when(s == 0)
+    def _():
+        ostage[...] = jnp.zeros_like(ostage)
+        zeros = pltpu.make_async_copy(ostage, next_o, loc_sem.at[0])
+        zeros.start()
+        zeros.wait()
+
+    @pl.when(s == SECTIONS - 1)
+    def _():
+        gstage[...] = jnp.zeros_like(gstage)
+        zeros = pltpu.make_async_copy(gstage, back_o, loc_sem.at[0])
+        zeros.start()
+        zeros.wait()
 
     ag_wait(rows(x, 1 - z), 0)
     ag_send(rows(x, 1 - z), rows(x, 1 - z), 3, 2, right)
@@ -251,40 +260,46 @@
     sib_wait(x2, 1 - z, 8, 0, HALF)
     sib_wait(x2, 1 - z, 9, HALF, HALF)
 
+    pl.semaphore_signal(ready.at[0], inc=1, device_id=(down, q), device_id_type=MESH)
+    pl.semaphore_signal(ready.at[1], inc=1, device_id=(up, q), device_id_type=MESH)
+
     hidden_group(x2, False, True)
-
-    def deal(stage, out, k, section):
-        def body(i, carry):
-            p = lax.rem(q + i, PEERS)
-            remote(
-                stage.at[pl.ds(pl.multiple_of(p * BLK, BLK), BLK)],
-                out.at[pl.ds(pl.multiple_of(q * BLK, BLK), BLK)],
-                a2a_ss.at[k], a2a_rs.at[k], (section, p),
-            ).start()
-            return carry
-
-        lax.fori_loop(0, PEERS, body, 0)
+    pl.semaphore_wait(ready.at[0], 1)
+
+    def send_block(stage, out, k, section, p):
+        remote(
+            stage.at[pl.ds(pl.multiple_of(p * BLK, BLK), BLK)],
+            out.at[pl.ds(pl.multiple_of(q * BLK, BLK), BLK)],
+            a2a_ss.at[k], a2a_rs.at[k], (section, p),
+        ).start()
 
     @pl.when(s < SECTIONS - 1)
     def _():
-        deal(ostage, next_o, 0, up)
+        def deal(i, carry):
+            send_block(ostage, next_o, 0, up, lax.rem(q + START + STRIDE * i, PEERS))
+            return carry
+
+        lax.fori_loop(0, PEERS, deal, 0)
 
     grad_group(x2)
+    pl.semaphore_wait(ready.at[1], 1)
 
     def grad_rows(i, carry):
-        r = pl.ds(pl.multiple_of(i * 16, 16), 16)
+        p = lax.rem(q + START + STRIDE * i, PEERS)
+        r = pl.ds(pl.multiple_of(p * BLK, BLK), BLK)
         wide = bperm[r].astype(F32)
         rstd = lax.rsqrt(jnp.mean(wide * wide, axis=-1, keepdims=True) + EPS)
         scaled = gain[...] * gn[r]
         inner = jnp.mean(wide * scaled, axis=-1, keepdims=True)
         gstage[r] = (cperm[r].astype(F32) + rstd * scaled - wide * (rstd * rstd * rstd * inner)).astype(BF16)
-        return carry
-
-    lax.fori_loop(0, TOK // 16, grad_rows, 0)
-
-    @pl.when(s > 0)
-    def _():
-        deal(gstage, back_o, 1, down)
+
+        @pl.when(s > 0)
+        def _():
+            send_block(gstage, back_o, 1, down, p)
+
+        return carry
+
+    lax.fori_loop(0, PEERS, grad_rows, 0)
 
     def slot(pz, pc):
         return cotq.at[pl.ds(pl.multiple_of(peer(0, pz, pc) * TOK, TOK), TOK)]
@@ -377,20 +392,6 @@
     @pl.when(s < SECTIONS - 1)
     def _():
         remote(gstage, back_o, a2a_ss.at[1], a2a_rs.at[1], sib).wait_recv()
-
-    @pl.when(s == 0)
-    def _():
-        nb[...] = jnp.zeros_like(nb)
-        cp = pltpu.make_async_copy(nb, next_o, loc_sem.at[0])
-        cp.start()
-        cp.wait()
-
-    @pl.when(s == SECTIONS - 1)
-    def _():
-        nb[...] = jnp.zeros_like(nb)
-        cp = pltpu.make_async_copy(nb, back_o, loc_sem.at[0])
-        cp.start()
-        cp.wait()
 
 
 def local(acts_fwd, acts_bwd, cot_bwd, gain, proj, fwd_route, bwd_route, straggler):
@@ -434,6 +435,7 @@
             dma((3,)), dma((3,)),
             dma((6,)), dma((6,)),
             dma((2,)), dma((2,)),
+            pltpu.SemaphoreType.REGULAR((2,)),
         ],
         compiler_params=pltpu.CompilerParams(
             collective_id=0, has_side_effects=True, vmem_limit_bytes=56 * 2**20
@@ -442,9 +444,46 @@
             flops=6 * TOK * C * C, bytes_accessed=20 * 2**20, transcendentals=0
         ),
     )(
-        acts_fwd[0], acts_bwd[0], cot_bwd[0], gain, proj[0], fwd_route[0], bwd_route[0], straggler
+        acts_fwd[0], acts_bwd[0], cot_bwd[0], gain, proj[0],
+        fwd_route.reshape(1, PEERS), bwd_route.reshape(1, PEERS), straggler,
     )
-    return tuple(o[None] for o in out)
+    return write_out(*out)
+
+
+PARTS = 4
+
+
+def write_kernel(a, b, w, ao, bo, wo, av, bv, wv, in_sem, out_sem):
+    moves = []
+    for k in range(PARTS):
+        for i, (src, buf, dst) in enumerate(((a, av, ao.at[0]), (b, bv, bo.at[0]), (w, wv, wo.at[0]))):
+            n = src.shape[0] // PARTS
+            at = pl.ds(k * n, n)
+            moves.append((
+                pltpu.make_async_copy(src.at[at], buf.at[at], in_sem.at[k, i]),
+                pltpu.make_async_copy(buf.at[at], dst.at[at], out_sem.at[k, i]),
+            ))
+    for read, _ in moves:
+        read.start()
+    for read, write in moves:
+        read.wait()
+        write.start()
+    for _, write in moves:
+        write.wait()
+
+
+def write_out(*results):
+    any_spec = pl.BlockSpec(memory_space=pl.ANY)
+    dma = pltpu.SemaphoreType.DMA
+    return pl.pallas_call(
+        write_kernel,
+        name="write_out",
+        out_shape=tuple(jax.ShapeDtypeStruct((1, *v.shape), v.dtype) for v in results),
+        in_specs=[any_spec] * 3,
+        out_specs=(any_spec,) * 3,
+        scratch_shapes=[pltpu.VMEM(v.shape, v.dtype) for v in results] + [dma((PARTS, 3)), dma((PARTS, 3))],
+        compiler_params=pltpu.CompilerParams(vmem_limit_bytes=56 * 2**20),
+    )(*results)
 
 
 def solution(mesh):

time: 151 us -> 140 us (0.927)
  the two profiles are of different devices: /device:TPU:39 before, /device:TPU:49 now
where the time goes in v2:
time: 140 us
  Pallas kernels  139 us (99%)
    pallas_call x1, Pallas kernels, local(): pl.pallas_call(kernel, name='swarm_tick', out_shape=(jax.ShapeDtypeStruct...  135 us
    pallas_call x1, Pallas kernels, write_out(): pl.pallas_call(write_kernel, name='write_out', out_shape=tuple((jax.Shape...  3.86 us

profile of v2, /device:TPU:49, one launch (start us, length us, event | category | flops | bytes accessed | tf_op | source)
XLA Modules:
  0.0 139.8 jit_solution(17021825907781983746)
XLA Ops:
  0.6 135.3 %swarm_tick.1 = (bf16[256,2560]{1,0:T(8,128)(2,1)}, bf16[256,2560]{1,0:T(8,128)(2,1)}, f32[160,2560]{1,0:T(8,128)}) custom-call(bf16[256,2560]{1,0:T(8,128)(2,1)} %bitcast.6, bf16[256,2560]{1,0:T(8,128)(2,1)} %bitcast.7, bf16[256,2560]{1,0:T(8,128)(2,1)} %bitcast.8, f32[1,2560]{1,0:T(1,128)} %gain.1, bf16[160,2560]{1,0:T(8,128)(2,1)} %bitcast.9, ...), custom_call_target="tpu_custom_call" | custom-call | flops 10066329600 | bytes 20971520 | tf_op jit(solution)/shard_map/swarm_tick/pallas_call | solution.py:402
  135.9 3.9 %write_out.1 = (bf16[1,256,2560]{2,1,0:T(8,128)(2,1)}, bf16[1,256,2560]{2,1,0:T(8,128)(2,1)}, f32[1,160,2560]{2,1,0:T(8,128)}) custom-call(bf16[256,2560]{1,0:T(8,128)(2,1)} %get-tuple-element.6.a, bf16[256,2560]{1,0:T(8,128)(2,1)} %get-tuple-element.7.b, f32[160,2560]{1,0:T(8,128)} %get-tuple-element.8.w), custom_call_target="tpu_custom_call" | custom-call | tf_op jit(solution)/shard_map/write_out/pallas_call | solution.py:478

commit v3 on v2

--- a/solution.py
+++ b/solution.py
@@ -56,9 +56,20 @@
     diag = (s, peer(x, 1 - z, 1 - c))
 
     bar = pltpu.get_barrier_semaphore()
-    for dev in (right, left, zpart, sib, diag, (up, q), (down, q)):
+    has_up = s < SECTIONS - 1
+    has_down = s > 0
+    for dev in (right, left, zpart, sib, diag):
         pl.semaphore_signal(bar, inc=1, device_id=dev, device_id_type=MESH)
-    pl.semaphore_wait(bar, 7)
+
+    @pl.when(has_up)
+    def _():
+        pl.semaphore_signal(bar, inc=1, device_id=(up, q), device_id_type=MESH)
+
+    @pl.when(has_down)
+    def _():
+        pl.semaphore_signal(bar, inc=1, device_id=(down, q), device_id_type=MESH)
+
+    pl.semaphore_wait(bar, 5 + has_up.astype(jnp.int32) + has_down.astype(jnp.int32))
 
     def remote(src, dst, ss, rs, dev):
         return pltpu.make_async_remote_copy(
@@ -260,11 +271,15 @@
     sib_wait(x2, 1 - z, 8, 0, HALF)
     sib_wait(x2, 1 - z, 9, HALF, HALF)
 
-    pl.semaphore_signal(ready.at[0], inc=1, device_id=(down, q), device_id_type=MESH)
-    pl.semaphore_signal(ready.at[1], inc=1, device_id=(up, q), device_id_type=MESH)
+    @pl.when(has_down)
+    def _():
+        pl.semaphore_signal(ready.at[0], inc=1, device_id=(down, q), device_id_type=MESH)
+
+    @pl.when(has_up)
+    def _():
+        pl.semaphore_signal(ready.at[1], inc=1, device_id=(up, q), device_id_type=MESH)
 
     hidden_group(x2, False, True)
-    pl.semaphore_wait(ready.at[0], 1)
 
     def send_block(stage, out, k, section, p):
         remote(
@@ -273,16 +288,20 @@
             a2a_ss.at[k], a2a_rs.at[k], (section, p),
         ).start()
 
-    @pl.when(s < SECTIONS - 1)
+    @pl.when(has_up)
     def _():
         def deal(i, carry):
             send_block(ostage, next_o, 0, up, lax.rem(q + START + STRIDE * i, PEERS))
             return carry
 
+        pl.semaphore_wait(ready.at[0], 1)
         lax.fori_loop(0, PEERS, deal, 0)
 
     grad_group(x2)
-    pl.semaphore_wait(ready.at[1], 1)
+
+    @pl.when(has_down)
+    def _():
+        pl.semaphore_wait(ready.at[1], 1)
 
     def grad_rows(i, carry):
         p = lax.rem(q + START + STRIDE * i, PEERS)
@@ -293,7 +312,7 @@
         inner = jnp.mean(wide * scaled, axis=-1, keepdims=True)
         gstage[r] = (cperm[r].astype(F32) + rstd * scaled - wide * (rstd * rstd * rstd * inner)).astype(BF16)
 
-        @pl.when(s > 0)
+        @pl.when(has_down)
         def _():
             send_block(gstage, back_o, 1, down, p)
 
@@ -377,19 +396,19 @@
     for cp in sent:
         cp.wait_send()
 
-    @pl.when(s < SECTIONS - 1)
+    @pl.when(has_up)
     def _():
         remote(ostage, next_o, a2a_ss.at[0], a2a_rs.at[0], sib).wait_send()
 
-    @pl.when(s > 0)
+    @pl.when(has_down)
     def _():
         remote(gstage, back_o, a2a_ss.at[1], a2a_rs.at[1], sib).wait_send()
 
-    @pl.when(s > 0)
+    @pl.when(has_down)
     def _():
         remote(ostage, next_o, a2a_ss.at[0], a2a_rs.at[0], sib).wait_recv()
 
-    @pl.when(s < SECTIONS - 1)
+    @pl.when(has_up)
     def _():
         remote(gstage, back_o, a2a_ss.at[1], a2a_rs.at[1], sib).wait_recv()
 
@@ -403,12 +422,12 @@
         kernel,
         name="swarm_tick",
         out_shape=(
-            jax.ShapeDtypeStruct((TOK, C), BF16),
-            jax.ShapeDtypeStruct((TOK, C), BF16),
-            jax.ShapeDtypeStruct((SH, C), F32),
+            pltpu.VMEM((TOK, C), BF16),
+            pltpu.VMEM((TOK, C), BF16),
+            pltpu.VMEM((SH, C), F32),
         ),
         in_specs=[hbm, hbm, hbm, vmem, hbm, vmem, vmem, smem],
-        out_specs=(hbm, hbm, vmem),
+        out_specs=(vmem, vmem, vmem),
         scratch_shapes=[
             pltpu.VMEM((C, C), BF16),
             pltpu.VMEM((TOK, C), BF16),
@@ -438,7 +457,7 @@
             pltpu.SemaphoreType.REGULAR((2,)),
         ],
         compiler_params=pltpu.CompilerParams(
-            collective_id=0, has_side_effects=True, vmem_limit_bytes=56 * 2**20
+            collective_id=0, has_side_effects=True, vmem_limit_bytes=53 * 2**20
         ),
         cost_estimate=pl.CostEstimate(
             flops=6 * TOK * C * C, bytes_accessed=20 * 2**20, transcendentals=0
@@ -453,36 +472,28 @@
 PARTS = 4
 
 
-def write_kernel(a, b, w, ao, bo, wo, av, bv, wv, in_sem, out_sem):
+def write_kernel(a, b, w, ao, bo, wo, sem):
     moves = []
     for k in range(PARTS):
-        for i, (src, buf, dst) in enumerate(((a, av, ao.at[0]), (b, bv, bo.at[0]), (w, wv, wo.at[0]))):
+        for i, (src, dst) in enumerate(((a, ao.at[0]), (b, bo.at[0]), (w, wo.at[0]))):
             n = src.shape[0] // PARTS
             at = pl.ds(k * n, n)
-            moves.append((
-                pltpu.make_async_copy(src.at[at], buf.at[at], in_sem.at[k, i]),
-                pltpu.make_async_copy(buf.at[at], dst.at[at], out_sem.at[k, i]),
-            ))
-    for read, _ in moves:
-        read.start()
-    for read, write in moves:
-        read.wait()
-        write.start()
-    for _, write in moves:
-        write.wait()
+            moves.append(pltpu.make_async_copy(src.at[at], dst.at[at], sem.at[k, i]))
+    for move in moves:
+        move.start()
+    for move in moves:
+        move.wait()
 
 
 def write_out(*results):
-    any_spec = pl.BlockSpec(memory_space=pl.ANY)
-    dma = pltpu.SemaphoreType.DMA
     return pl.pallas_call(
         write_kernel,
         name="write_out",
         out_shape=tuple(jax.ShapeDtypeStruct((1, *v.shape), v.dtype) for v in results),
-        in_specs=[any_spec] * 3,
-        out_specs=(any_spec,) * 3,
-        scratch_shapes=[pltpu.VMEM(v.shape, v.dtype) for v in results] + [dma((PARTS, 3)), dma((PARTS, 3))],
-        compiler_params=pltpu.CompilerParams(vmem_limit_bytes=56 * 2**20),
+        in_specs=[pl.BlockSpec(memory_space=pltpu.VMEM)] * 3,
+        out_specs=(pl.BlockSpec(memory_space=pl.ANY),) * 3,
+        scratch_shapes=[pltpu.SemaphoreType.DMA((PARTS, 3))],
+        compiler_params=pltpu.CompilerParams(vmem_limit_bytes=8 * 2**20),
     )(*results)
 
 

time: 140 us -> 138 us (0.986)
  Pallas kernels: 139 us -> 137 us
    pallas_call x1, Pallas kernels: 3.86 us -> 2.12 us  [write_out(): pl.pallas_call(write_kernel, name='write_out', out_shape=tuple((jax.Shape...]
where the time goes in v3:
time: 138 us; the launch traced here: 137 us
  Pallas kernels  137 us (99%)
    pallas_call x1, Pallas kernels, local(): pl.pallas_call(kernel, name='swarm_tick', out_shape=(pltpu.VMEM((TOK, C),...  135 us

profile of v3, /device:TPU:49, one launch (start us, length us, event | category | flops | bytes accessed | tf_op | source)
XLA Modules:
  0.0 137.4 jit_solution(17717042551189783701)
XLA Ops:
  0.6 134.6 %swarm_tick.1 = (bf16[256,2560]{1,0:T(8,128)(2,1)S(1)}, bf16[256,2560]{1,0:T(8,128)(2,1)S(1)}, f32[160,2560]{1,0:T(8,128)S(1)}) custom-call(bf16[256,2560]{1,0:T(8,128)(2,1)} %bitcast.6, bf16[256,2560]{1,0:T(8,128)(2,1)} %bitcast.7, bf16[256,2560]{1,0:T(8,128)(2,1)} %bitcast.8, f32[1,2560]{1,0:T(1,128)} %gain.1, bf16[160,2560]{1,0:T(8,128)(2,1)} %bitcast.9, ...), custom_call_target="tpu_custom_call" | custom-call | flops 10066329600 | bytes 20971520 | tf_op jit(solution)/shard_map/swarm_tick/pallas_call | solution.py:421
  135.3 2.1 %write_out.1 = (bf16[1,256,2560]{2,1,0:T(8,128)(2,1)}, bf16[1,256,2560]{2,1,0:T(8,128)(2,1)}, f32[1,160,2560]{2,1,0:T(8,128)}) custom-call(bf16[256,2560]{1,0:T(8,128)(2,1)S(1)} %get-tuple-element.6.a, bf16[256,2560]{1,0:T(8,128)(2,1)S(1)} %get-tuple-element.7.b, f32[160,2560]{1,0:T(8,128)S(1)} %get-tuple-element.8.w), custom_call_target="tpu_custom_call" | custom-call | tf_op jit(solution)/shard_map/write_out/pallas_call | solution.py:489

commit v4 on v3

--- a/solution.py
+++ b/solution.py
@@ -32,7 +32,7 @@
     next_o, back_o, dw_o,
     wg, af, ab, aperm, bperm, cperm, na, nb, nbt, nbq, cotq, hacc, gn, ostage, gstage,
     psend, rs_half, rs_full,
-    loc_sem, ag_ss, ag_rs, sib_ss, sib_rs, ex_ss, ex_rs, nb_ss, nb_rs, red_ss, red_rs, a2a_ss, a2a_rs, ready,
+    loc_sem, ag_ss, ag_rs, sib_ss, sib_rs, ex_ss, ex_rs, nb_ss, nb_rs, red_ss, red_rs, a2a_ss, a2a_rs, ready, hello,
 ):
     s = lax.axis_index("section")
     q = lax.axis_index("peer")
@@ -61,15 +61,32 @@
     for dev in (right, left, zpart, sib, diag):
         pl.semaphore_signal(bar, inc=1, device_id=dev, device_id_type=MESH)
 
-    @pl.when(has_up)
-    def _():
-        pl.semaphore_signal(bar, inc=1, device_id=(up, q), device_id_type=MESH)
-
-    @pl.when(has_down)
-    def _():
-        pl.semaphore_signal(bar, inc=1, device_id=(down, q), device_id_type=MESH)
-
-    pl.semaphore_wait(bar, 5 + has_up.astype(jnp.int32) + has_down.astype(jnp.int32))
+    even = lax.rem(s, 2) == 0
+    odd = lax.rem(s, 2) == 1
+
+    @pl.when(even)
+    def _():
+        pl.semaphore_wait(bar, 5)
+
+        @pl.when(has_up)
+        def _():
+            pl.semaphore_signal(bar, inc=1, device_id=(up, q), device_id_type=MESH)
+
+        @pl.when(has_down)
+        def _():
+            pl.semaphore_signal(bar, inc=1, device_id=(down, q), device_id_type=MESH)
+
+    @pl.when(odd)
+    def _():
+        pl.semaphore_wait(bar, 5 + has_up.astype(jnp.int32) + has_down.astype(jnp.int32))
+
+        @pl.when(has_up)
+        def _():
+            pl.semaphore_signal(hello.at[1], inc=1, device_id=(up, q), device_id_type=MESH)
+
+        @pl.when(has_down)
+        def _():
+            pl.semaphore_signal(hello.at[0], inc=1, device_id=(down, q), device_id_type=MESH)
 
     def remote(src, dst, ss, rs, dev):
         return pltpu.make_async_remote_copy(
@@ -271,6 +288,14 @@
     sib_wait(x2, 1 - z, 8, 0, HALF)
     sib_wait(x2, 1 - z, 9, HALF, HALF)
 
+    @pl.when(even & has_up)
+    def _():
+        pl.semaphore_wait(hello.at[0], 1)
+
+    @pl.when(even & has_down)
+    def _():
+        pl.semaphore_wait(hello.at[1], 1)
+
     @pl.when(has_down)
     def _():
         pl.semaphore_signal(ready.at[0], inc=1, device_id=(down, q), device_id_type=MESH)
@@ -280,6 +305,10 @@
         pl.semaphore_signal(ready.at[1], inc=1, device_id=(up, q), device_id_type=MESH)
 
     hidden_group(x2, False, True)
+
+    def offset_peer(i):
+        j = lax.rem(i, 4)
+        return lax.rem(q + 4 * (2 + 2 * j + lax.div(j, 2)) + lax.div(i, 4), PEERS)
 
     def send_block(stage, out, k, section, p):
         remote(
@@ -291,7 +320,7 @@
     @pl.when(has_up)
     def _():
         def deal(i, carry):
-            send_block(ostage, next_o, 0, up, lax.rem(q + START + STRIDE * i, PEERS))
+            send_block(ostage, next_o, 0, up, offset_peer(i))
             return carry
 
         pl.semaphore_wait(ready.at[0], 1)
@@ -304,7 +333,7 @@
         pl.semaphore_wait(ready.at[1], 1)
 
     def grad_rows(i, carry):
-        p = lax.rem(q + START + STRIDE * i, PEERS)
+        p = offset_peer(i)
         r = pl.ds(pl.multiple_of(p * BLK, BLK), BLK)
         wide = bperm[r].astype(F32)
         rstd = lax.rsqrt(jnp.mean(wide * wide, axis=-1, keepdims=True) + EPS)
@@ -454,6 +483,7 @@
             dma((3,)), dma((3,)),
             dma((6,)), dma((6,)),
             dma((2,)), dma((2,)),
+            pltpu.SemaphoreType.REGULAR((2,)),
             pltpu.SemaphoreType.REGULAR((2,)),
         ],
         compiler_params=pltpu.CompilerParams(

time: 138 us -> 136 us (0.986); the launches traced: 137 us -> 133 us
  Pallas kernels: 137 us -> 133 us
    pallas_call x1, Pallas kernels: 135 us -> 131 us  [local(): pl.pallas_call(kernel, name='swarm_tick', out_shape=(pltpu.VMEM((TOK, C),...]
where the time goes in v4:
time: 136 us; the launch traced here: 133 us
  Pallas kernels  133 us (98%)
    pallas_call x1, Pallas kernels, local(): pl.pallas_call(kernel, name='swarm_tick', out_shape=(pltpu.VMEM((TOK, C),...  131 us

profile of v4, /device:TPU:49, one launch (start us, length us, event | category | flops | bytes accessed | tf_op | source)
XLA Modules:
  0.0 133.4 jit_solution(17357616429582131418)
XLA Ops:
  0.6 130.6 %swarm_tick.1 = (bf16[256,2560]{1,0:T(8,128)(2,1)S(1)}, bf16[256,2560]{1,0:T(8,128)(2,1)S(1)}, f32[160,2560]{1,0:T(8,128)S(1)}) custom-call(bf16[256,2560]{1,0:T(8,128)(2,1)} %bitcast.6, bf16[256,2560]{1,0:T(8,128)(2,1)} %bitcast.7, bf16[256,2560]{1,0:T(8,128)(2,1)} %bitcast.8, f32[1,2560]{1,0:T(1,128)} %gain.1, bf16[160,2560]{1,0:T(8,128)(2,1)} %bitcast.9, ...), custom_call_target="tpu_custom_call" | custom-call | flops 10066329600 | bytes 20971520 | tf_op jit(solution)/shard_map/swarm_tick/pallas_call | solution.py:450
  131.2 2.1 %write_out.1 = (bf16[1,256,2560]{2,1,0:T(8,128)(2,1)}, bf16[1,256,2560]{2,1,0:T(8,128)(2,1)}, f32[1,160,2560]{2,1,0:T(8,128)}) custom-call(bf16[256,2560]{1,0:T(8,128)(2,1)S(1)} %get-tuple-element.6.a, bf16[256,2560]{1,0:T(8,128)(2,1)S(1)} %get-tuple-element.7.b, f32[160,2560]{1,0:T(8,128)S(1)} %get-tuple-element.8.w), custom_call_target="tpu_custom_call" | custom-call | tf_op jit(solution)/shard_map/write_out/pallas_call | solution.py:519

commit v5 on v4

--- a/solution.py
+++ b/solution.py
@@ -116,7 +116,8 @@
         region = rows(px, pz, lo, n, 1 - c)
         remote(region, region, sib_ss.at[k], sib_rs.at[k], sib).wait_recv()
 
-    ag_send(proj, rows(x, z), 0, 0, zpart)
+    ag_send(proj.at[pl.ds(0, HALF)], rows(x, z, 0, HALF), 0, 0, zpart)
+    ag_send(proj.at[pl.ds(HALF, HALF)], rows(x, z, HALF, HALF), 9, 9, zpart)
     ag_send(proj, rows(x, z), 1, 1, right)
     ag_send(proj, rows(x, z), 2, 5, left)
     sib_send(proj, rows(x, z), 0)
@@ -161,6 +162,14 @@
     send(nbt.at[nb_sib], nbq.at[quad], nb_ss.at[0], nb_rs.at[0], sib)
     nbq[quad] = nbt[quad]
 
+    def pass_on(half, k_recv, k_send, k_left, k_right):
+        part = rows(x, 1 - z, half * HALF, HALF)
+        ag_wait(part, k_recv)
+        ag_send(part, part, k_send, k_left, right)
+        ag_send(part, part, k_send + 1, k_right, left)
+
+    pass_on(0, 0, 3, 2, 6)
+
     def ordering(route_ref):
         st = (route_ref[...] == lax.broadcasted_iota(jnp.int32, (PEERS, PEERS), 0)).astype(F32).astype(BF16)
         e = ((lax.broadcasted_iota(jnp.int32, (TOK, PEERS), 0) >> 4)
@@ -210,9 +219,7 @@
         zeros.start()
         zeros.wait()
 
-    ag_wait(rows(x, 1 - z), 0)
-    ag_send(rows(x, 1 - z), rows(x, 1 - z), 3, 2, right)
-    ag_send(rows(x, 1 - z), rows(x, 1 - z), 4, 6, left)
+    pass_on(1, 9, 10, 10, 11)
     sib_send(rows(x, 1 - z), rows(x, 1 - z), 1)
     send(cot, cotq.at[own_slot], ex_ss.at[1], ex_rs.at[1], zpart)
     send(nbt.at[nb_z], nbq.at[quad], nb_ss.at[1], nb_rs.at[1], zpart)
@@ -259,12 +266,14 @@
     hidden_group(x, True, False)
     grad_group(x)
 
-    ag_wait(rows(xl, 1 - z), 2)
+    ag_wait(rows(xl, 1 - z, 0, HALF), 2)
     ag_send(rows(xl, 1 - z, 0, HALF), rows(xl, 1 - z, 0, HALF), 7, 4, right)
-    sib_send(rows(xl, 1 - z), rows(xl, 1 - z), 4)
-    ag_wait(rows(xr, 1 - z), 6)
+    ag_wait(rows(xr, 1 - z, 0, HALF), 6)
+    ag_wait(rows(xr, 1 - z, HALF, HALF), 11)
     ag_send(rows(xr, 1 - z, HALF, HALF), rows(xr, 1 - z, HALF, HALF), 8, 8, left)
     sib_send(rows(xr, 1 - z), rows(xr, 1 - z), 5)
+    ag_wait(rows(xl, 1 - z, HALF, HALF), 10)
+    sib_send(rows(xl, 1 - z), rows(xl, 1 - z), 4)
 
     sib_wait(xl, z, 2)
     sib_wait(xl, 1 - z, 4)
@@ -307,8 +316,10 @@
     hidden_group(x2, False, True)
 
     def offset_peer(i):
-        j = lax.rem(i, 4)
-        return lax.rem(q + 4 * (2 + 2 * j + lax.div(j, 2)) + lax.div(i, 4), PEERS)
+        j = lax.rem(i, 2)
+        late = lax.div(i, 8)
+        k = lax.rem(lax.div(i, 2), 4)
+        return lax.rem(q + 4 * (2 + 2 * j + late) + k, PEERS)
 
     def send_block(stage, out, k, section, p):
         remote(
@@ -477,7 +488,7 @@
             pltpu.VMEM((2, HALF, C), BF16),
             pltpu.VMEM((2, SH, C), BF16),
             dma((4,)),
-            dma((9,)), dma((9,)),
+            dma((12,)), dma((12,)),
             dma((10,)), dma((10,)),
             dma((3,)), dma((3,)),
             dma((3,)), dma((3,)),

time: 136 us -> 135 us (level)
  no operation moved by 1% of the time
where the time goes in v5:
time: 135 us; the launch traced here: 133 us
  Pallas kernels  133 us (99%)
    pallas_call x1, Pallas kernels, local(): pl.pallas_call(kernel, name='swarm_tick', out_shape=(pltpu.VMEM((TOK, C),...  130 us

profile of v5, /device:TPU:49, one launch (start us, length us, event | category | flops | bytes accessed | tf_op | source)
XLA Modules:
  0.0 133.2 jit_solution(4982577889329059054)
XLA Ops:
  0.6 130.5 %swarm_tick.1 = (bf16[256,2560]{1,0:T(8,128)(2,1)S(1)}, bf16[256,2560]{1,0:T(8,128)(2,1)S(1)}, f32[160,2560]{1,0:T(8,128)S(1)}) custom-call(bf16[256,2560]{1,0:T(8,128)(2,1)} %bitcast.6, bf16[256,2560]{1,0:T(8,128)(2,1)} %bitcast.7, bf16[256,2560]{1,0:T(8,128)(2,1)} %bitcast.8, f32[1,2560]{1,0:T(1,128)} %gain.1, bf16[160,2560]{1,0:T(8,128)(2,1)} %bitcast.9, ...), custom_call_target="tpu_custom_call" | custom-call | flops 10066329600 | bytes 20971520 | tf_op jit(solution)/shard_map/swarm_tick/pallas_call | solution.py:461
  131.1 2.1 %write_out.1 = (bf16[1,256,2560]{2,1,0:T(8,128)(2,1)}, bf16[1,256,2560]{2,1,0:T(8,128)(2,1)}, f32[1,160,2560]{2,1,0:T(8,128)}) custom-call(bf16[256,2560]{1,0:T(8,128)(2,1)S(1)} %get-tuple-element.6.a, bf16[256,2560]{1,0:T(8,128)(2,1)S(1)} %get-tuple-element.7.b, f32[160,2560]{1,0:T(8,128)S(1)} %get-tuple-element.8.w), custom_call_target="tpu_custom_call" | custom-call | tf_op jit(solution)/shard_map/write_out/pallas_call | solution.py:530

commit v6 on v5

--- a/solution.py
+++ b/solution.py
@@ -169,6 +169,7 @@
         ag_send(part, part, k_send + 1, k_right, left)
 
     pass_on(0, 0, 3, 2, 6)
+    send(cot, cotq.at[own_slot], ex_ss.at[1], ex_rs.at[1], zpart)
 
     def ordering(route_ref):
         st = (route_ref[...] == lax.broadcasted_iota(jnp.int32, (PEERS, PEERS), 0)).astype(F32).astype(BF16)
@@ -221,7 +222,6 @@
 
     pass_on(1, 9, 10, 10, 11)
     sib_send(rows(x, 1 - z), rows(x, 1 - z), 1)
-    send(cot, cotq.at[own_slot], ex_ss.at[1], ex_rs.at[1], zpart)
     send(nbt.at[nb_z], nbq.at[quad], nb_ss.at[1], nb_rs.at[1], zpart)
     send(nbt.at[nb_diag], nbq.at[quad], nb_ss.at[2], nb_rs.at[2], diag)
 

time: 135 us -> 134 us (level)
  Pallas kernels: 133 us -> 131 us
    pallas_call x1, Pallas kernels: 130 us -> 129 us  [local(): pl.pallas_call(kernel, name='swarm_tick', out_shape=(pltpu.VMEM((TOK, C),...]
where the time goes in v6:
time: 134 us; the launch traced here: 132 us
  Pallas kernels  131 us (98%)
    pallas_call x1, Pallas kernels, local(): pl.pallas_call(kernel, name='swarm_tick', out_shape=(pltpu.VMEM((TOK, C),...  129 us

profile of v6, /device:TPU:49, one launch (start us, length us, event | category | flops | bytes accessed | tf_op | source)
XLA Modules:
  0.0 131.8 jit_solution(6654701259029803696)
XLA Ops:
  0.6 129.1 %swarm_tick.1 = (bf16[256,2560]{1,0:T(8,128)(2,1)S(1)}, bf16[256,2560]{1,0:T(8,128)(2,1)S(1)}, f32[160,2560]{1,0:T(8,128)S(1)}) custom-call(bf16[256,2560]{1,0:T(8,128)(2,1)} %bitcast.6, bf16[256,2560]{1,0:T(8,128)(2,1)} %bitcast.7, bf16[256,2560]{1,0:T(8,128)(2,1)} %bitcast.8, f32[1,2560]{1,0:T(1,128)} %gain.1, bf16[160,2560]{1,0:T(8,128)(2,1)} %bitcast.9, ...), custom_call_target="tpu_custom_call" | custom-call | flops 10066329600 | bytes 20971520 | tf_op jit(solution)/shard_map/swarm_tick/pallas_call | solution.py:461
  129.7 2.1 %write_out.1 = (bf16[1,256,2560]{2,1,0:T(8,128)(2,1)}, bf16[1,256,2560]{2,1,0:T(8,128)(2,1)}, f32[1,160,2560]{2,1,0:T(8,128)}) custom-call(bf16[256,2560]{1,0:T(8,128)(2,1)S(1)} %get-tuple-element.6.a, bf16[256,2560]{1,0:T(8,128)(2,1)S(1)} %get-tuple-element.7.b, f32[160,2560]{1,0:T(8,128)S(1)} %get-tuple-element.8.w), custom_call_target="tpu_custom_call" | custom-call | tf_op jit(solution)/shard_map/write_out/pallas_call | solution.py:530
